TPU v7x, 32 devices: a whole 2x2x4 slice. The times are simulated.
32 devices in a mesh: section: 2 (over x), clip: 4 (over y, core), seq: 4 (over z).
Axes of the slice: x: 2, y: 2, z: 4, core: 2. Of those that a mesh axis runs over, the one named last changes fastest.
Arguments:
- ends_in: bfloat16 [2, 2, 4, 256, 768], P('section', None, 'clip', 'seq'), may hold values from -6 to 6
- clip_counts: int32 [2], replicated, may hold values from 1 to 4, as said below
- qkv_weight: bfloat16 [2, 768, 2304], P('section', ('clip', 'seq')), may hold values from -0.21875 to 0.21875
- out_weight: bfloat16 [2, 768, 768], P('section', ('clip', 'seq')), may hold values from -0.875 to 0.875
- up_weight: bfloat16 [2, 768, 3072], P('section', ('clip', 'seq')), may hold values from -0.21875 to 0.21875
- down_weight: bfloat16 [2, 3072, 768], P('section', ('clip', 'seq')), may hold values from -0.109375 to 0.109375
- norm_gains: bfloat16 [2, 2, 768], P('section', None, ('clip', 'seq')), may hold values from 0.099609375 to 1.8984375
- vec_bias: bfloat16 [2, 6, 768], P('section', None, ('clip', 'seq')), may hold values from -2 to 2
- up_bias: bfloat16 [2, 3072], P('section', ('clip', 'seq')), may hold values from -2 to 2
Outputs:
- ends_out: float32 [2, 2, 4, 256, 768], P('section', None, 'clip', 'seq')
- qkv_grad: float32 [2, 768, 2304], P('section', ('clip', 'seq'))
- out_grad: float32 [2, 768, 768], P('section', ('clip', 'seq'))
- up_grad: float32 [2, 768, 3072], P('section', ('clip', 'seq'))
- down_grad: float32 [2, 3072, 768], P('section', ('clip', 'seq'))
- gains_grad: float32 [2, 2, 768], P('section', None, ('clip', 'seq'))
- bias_grad: float32 [2, 6, 768], P('section', None, ('clip', 'seq'))
- up_bias_grad: float32 [2, 3072], P('section', ('clip', 'seq'))
Inputs may be any that keep to these rules, and one draw needn't show every extreme that they name: clip_counts is 4 for every micro-batch but one, which holds fewer valid clips: its first clip_counts[m] slots.
All inputs are finite; a program needn't handle non-finite values.
Results may differ from a plain program's by a relative error of at most 0.017.
Values may be sent and summed in bfloat16 or wider, within the bound.
A program may use at most 192 MiB of HBM per device.

v0:
```python
import jax
import jax.numpy as jnp
from jax import lax
from jax.sharding import PartitionSpec as P

HEAD_DIM = 64


def from_behind(block, axis, distance):
    devices = range(lax.axis_size(axis))
    route = [(i - distance, i) for i in devices if i - distance in devices]
    return lax.ppermute(block, axis, route)


def gelu_exact(values):
    return jax.nn.gelu(values, approximate=False)


def norm_parts(values):
    centered = values - jnp.mean(values, axis=-1, keepdims=True)
    inverse = lax.rsqrt(jnp.mean(centered * centered, axis=-1, keepdims=True) + 1e-05)
    return (centered * inverse, inverse)


def norm_back(grad_hat, normal, inverse):
    first_term = grad_hat - jnp.mean(grad_hat, axis=-1, keepdims=True)
    return inverse * (first_term - normal * jnp.mean(grad_hat * normal, axis=-1, keepdims=True))


def matmul(left, right):
    return jnp.dot(left, right, preferred_element_type=jnp.float32)


def times_transposed(left, right):
    return lax.dot_general(
        left, right, (((1,), (1,)), ((), ())), preferred_element_type=jnp.float32
    )


def transposed_times(left, right):
    return lax.dot_general(
        left, right, (((0,), (0,)), ((), ())), preferred_element_type=jnp.float32
    )


def attention_scores(query_heads, key_heads):
    scores = jnp.einsum(
        "cqhd,ckhd->chqk", query_heads, key_heads, preferred_element_type=jnp.float32
    )
    return scores * HEAD_DIM ** (-0.5)


def split_heads(rows):
    return rows.reshape(rows.shape[0], rows.shape[1], rows.shape[2] // HEAD_DIM, HEAD_DIM)


def layer_forward(layer_in, weights):
    qkv_weight, out_weight, up_weight, down_weight, gain_rows, shifts, up_shift = weights
    gain_rows = gain_rows.astype(jnp.float32)
    shifts = shifts.astype(jnp.float32)
    clip_count, frames, model_width = layer_in.shape
    row_data = layer_in.reshape(clip_count * frames, model_width).astype(jnp.float32)
    normal_one, inverse_one = norm_parts(row_data)
    normed_one = (normal_one * gain_rows[0] + shifts[0]).astype(jnp.bfloat16)
    projected = matmul(normed_one, qkv_weight)
    query_rows = (
        (projected[:, :model_width] + shifts[2])
        .astype(jnp.bfloat16)
        .reshape(clip_count, frames, model_width)
    )
    key_rows = projected[:, model_width : 2 * model_width].astype(jnp.bfloat16)
    value_rows = (projected[:, 2 * model_width :] + shifts[3]).astype(jnp.bfloat16)
    all_keys, all_values = (
        lax.all_gather(
            key_rows.reshape(clip_count, frames, model_width), "seq", axis=1, tiled=True
        ),
        lax.all_gather(
            value_rows.reshape(clip_count, frames, model_width), "seq", axis=1, tiled=True
        ),
    )
    value_heads = split_heads(all_values)
    scores = attention_scores(split_heads(query_rows), split_heads(all_keys))
    row_max = jnp.max(scores, axis=-1, keepdims=True)
    log_total = row_max + jnp.log(jnp.sum(jnp.exp(scores - row_max), axis=-1, keepdims=True))
    attn_probs = jnp.exp(scores - log_total).astype(jnp.bfloat16)
    mixed_rows = jnp.einsum(
        "chqk,ckhd->cqhd", attn_probs, value_heads, preferred_element_type=jnp.float32
    )
    mixed_rows = mixed_rows.reshape(clip_count * frames, model_width).astype(jnp.bfloat16)
    hidden = row_data + matmul(mixed_rows, out_weight) + shifts[4]
    normal_two, inverse_two = norm_parts(hidden)
    normed_two = (normal_two * gain_rows[1] + shifts[1]).astype(jnp.bfloat16)
    before = matmul(normed_two, up_weight) + up_shift.astype(jnp.float32)
    activated = gelu_exact(before).astype(jnp.bfloat16)
    result = hidden + matmul(activated, down_weight) + shifts[5]
    kept_data = (
        layer_in,
        normed_one,
        query_rows,
        all_keys,
        all_values,
        log_total[..., 0],
        mixed_rows,
        hidden,
        normed_two,
        before,
        activated,
    )
    return (result.reshape(clip_count, frames, model_width), kept_data)


def layer_backward(grad_out, kept_data, weights):
    qkv_weight, out_weight, up_weight, down_weight, gain_rows, shifts, up_shift = weights
    gain_rows = gain_rows.astype(jnp.float32)
    (
        layer_in,
        normed_one,
        query_rows,
        all_keys,
        all_values,
        log_total,
        mixed_rows,
        hidden,
        normed_two,
        before,
        activated,
    ) = kept_data
    clip_count, frames, model_width = layer_in.shape
    row_count = clip_count * frames
    query_heads = split_heads(query_rows)
    key_heads = split_heads(all_keys)
    value_heads = split_heads(all_values)
    row_data = layer_in.reshape(row_count, model_width).astype(jnp.float32)
    normal_one, inverse_one = norm_parts(row_data)
    normal_two, inverse_two = norm_parts(hidden)
    grad_rows = grad_out.reshape(row_count, model_width)
    down_grad = grad_rows.astype(jnp.bfloat16)
    act_grad = times_transposed(down_grad, down_weight)
    up_grad = jax.vjp(gelu_exact, before)[1](act_grad)[0].astype(jnp.bfloat16)
    norm_two_grad = times_transposed(up_grad, up_weight)
    hidden_grad = grad_rows + norm_back(norm_two_grad * gain_rows[1], normal_two, inverse_two)
    branch_grad = hidden_grad.astype(jnp.bfloat16)
    mixed_grad = times_transposed(branch_grad, out_weight).astype(jnp.bfloat16)
    mixed_heads = mixed_grad.reshape(query_heads.shape)
    scores = attention_scores(query_heads, key_heads)
    soft_probs = jnp.exp(scores - log_total[..., None])
    probs_grad = jnp.einsum(
        "cqhd,ckhd->chqk", mixed_heads, value_heads, preferred_element_type=jnp.float32
    )
    row_delta = jnp.sum(soft_probs * probs_grad, axis=-1)
    score_grad = (soft_probs * (probs_grad - row_delta[..., None])).astype(jnp.bfloat16)
    score_scale = HEAD_DIM ** (-0.5)
    query_grad = (
        jnp.einsum("chqk,ckhd->cqhd", score_grad, key_heads, preferred_element_type=jnp.float32)
        * score_scale
    )
    key_part = (
        jnp.einsum("chqk,cqhd->ckhd", score_grad, query_heads, preferred_element_type=jnp.float32)
        * score_scale
    )
    value_part = jnp.einsum(
        "chqk,cqhd->ckhd",
        soft_probs.astype(jnp.bfloat16),
        mixed_heads,
        preferred_element_type=jnp.float32,
    )
    total_length = key_heads.shape[1]
    key_grad, value_grad = (
        lax.psum_scatter(
            key_part.reshape(clip_count, total_length, model_width).astype(jnp.bfloat16),
            "seq",
            scatter_dimension=1,
            tiled=True,
        ).astype(jnp.float32),
        lax.psum_scatter(
            value_part.reshape(clip_count, total_length, model_width).astype(jnp.bfloat16),
            "seq",
            scatter_dimension=1,
            tiled=True,
        ).astype(jnp.float32),
    )
    qkv_grad = jnp.concatenate(
        [
            query_grad.reshape(row_count, model_width),
            key_grad.reshape(row_count, model_width),
            value_grad.reshape(row_count, model_width),
        ],
        axis=1,
    ).astype(jnp.bfloat16)
    norm_one_grad = times_transposed(qkv_grad, qkv_weight)
    input_grad = hidden_grad + norm_back(norm_one_grad * gain_rows[0], normal_one, inverse_one)
    operands = (
        normed_one,
        qkv_grad,
        mixed_rows,
        branch_grad,
        normed_two,
        up_grad,
        activated,
        down_grad,
    )
    small_sums = (
        jnp.sum(norm_one_grad * normal_one, axis=0),
        jnp.sum(norm_two_grad * normal_two, axis=0),
        jnp.sum(norm_one_grad, axis=0),
        jnp.sum(norm_two_grad, axis=0),
    )
    return (input_grad.reshape(clip_count, frames, model_width), operands, small_sums)


def on_device(
    ends_in,
    clip_counts,
    qkv_weight,
    out_weight,
    up_weight,
    down_weight,
    norm_gains,
    vec_bias,
    up_bias,
):
    local_shards = (
        qkv_weight[0],
        out_weight[0],
        up_weight[0],
        down_weight[0],
        norm_gains[0],
        vec_bias[0],
        up_bias[0],
    )
    weights = (
        lax.all_gather(local_shards[0], ("clip", "seq"), axis=0, tiled=True),
        lax.all_gather(local_shards[1], ("clip", "seq"), axis=0, tiled=True),
        lax.all_gather(local_shards[2], ("clip", "seq"), axis=0, tiled=True),
        lax.all_gather(local_shards[3], ("clip", "seq"), axis=0, tiled=True),
        lax.all_gather(local_shards[4], ("clip", "seq"), axis=1, tiled=True),
        lax.all_gather(local_shards[5], ("clip", "seq"), axis=1, tiled=True),
        lax.all_gather(local_shards[6], ("clip", "seq"), axis=0, tiled=True),
    )
    section_first = lax.axis_index("section") == 0
    ends_local = ends_in[0]
    batch_count, clip_count, frames, model_width = ends_local.shape
    total_steps = batch_count + 1
    zero_block = jnp.zeros((clip_count, frames, model_width), jnp.bfloat16)
    received = zero_block
    kept_list = []
    top_list = []
    for step_index in range(total_steps):
        fresh_block = ends_local[step_index] if step_index < batch_count else zero_block
        layer_in = jnp.where(section_first, fresh_block, received)
        layer_out, kept_data = layer_forward(layer_in, weights)
        kept_list.append(kept_data)
        if step_index >= 1:
            top_list.append(layer_out)
        if step_index < batch_count:
            received = from_behind(layer_out.astype(jnp.bfloat16), "section", 1)
    kept_stack = tuple(
        (
            jnp.stack([entry_data[item_index] for entry_data in kept_list])
            for item_index in range(len(kept_list[0]))
        )
    )
    clip_ids = lax.axis_index("clip") * clip_count + jnp.arange(clip_count, dtype=jnp.int32)
    received = zero_block
    operand_list = []
    small_list = []
    input_list = []
    for step_index in range(total_steps):
        if step_index < batch_count:
            valid_rows = (clip_ids < clip_counts[step_index]).astype(jnp.bfloat16)
            fresh_block = ends_local[step_index] * valid_rows[:, None, None]
        else:
            fresh_block = zero_block
        grad_out = jnp.where(section_first, received, fresh_block).astype(jnp.float32)
        position = jnp.clip(
            jnp.where(section_first, step_index - 1, step_index + 1), 0, total_steps - 1
        )
        kept_data = tuple(
            (
                lax.dynamic_index_in_dim(entry_data, position, 0, keepdims=False)
                for entry_data in kept_stack
            )
        )
        input_grad, operands, small_sums = layer_backward(grad_out, kept_data, weights)
        operand_list.append(operands)
        small_list.append(small_sums)
        if step_index >= 1:
            input_list.append(input_grad)
        if step_index < batch_count:
            received = from_behind(input_grad.astype(jnp.bfloat16), "section", -1)
    joined = [
        jnp.concatenate([entry_data[item_index] for entry_data in operand_list], axis=0)
        for item_index in range(8)
    ]
    small_total = [
        jnp.sum(jnp.stack([entry_data[item_index] for entry_data in small_list]), axis=0)
        for item_index in range(4)
    ]
    qkv_bias = jnp.sum(joined[1], axis=0, dtype=jnp.float32)
    branch_bias = jnp.sum(joined[3], axis=0, dtype=jnp.float32)
    down_bias = jnp.sum(joined[7], axis=0, dtype=jnp.float32)
    small_columns = jnp.stack(
        [
            small_total[0],
            small_total[1],
            small_total[2],
            small_total[3],
            qkv_bias[:model_width],
            qkv_bias[2 * model_width :],
            branch_bias,
            down_bias,
        ],
        axis=1,
    )
    up_shift_total = jnp.sum(joined[5], axis=0, dtype=jnp.float32)
    ff_width = joined[5].shape[1]
    first_left = joined[0]
    second_left = joined[2]
    third_left = joined[4]
    model_summed = lax.psum_scatter(
        jnp.concatenate(
            [
                transposed_times(first_left, joined[1]),
                transposed_times(second_left, joined[3]),
                transposed_times(third_left, joined[5]),
                small_columns,
            ],
            axis=1,
        ),
        ("clip", "seq"),
        scatter_dimension=0,
        tiled=True,
    )
    unit_left = joined[6]
    unit_summed = lax.psum_scatter(
        jnp.concatenate([transposed_times(unit_left, joined[7]), up_shift_total[:, None]], axis=1),
        ("clip", "seq"),
        scatter_dimension=0,
        tiled=True,
    )
    qkv_part = model_summed[:, : 3 * model_width]
    out_part = model_summed[:, 3 * model_width : 4 * model_width]
    up_part = model_summed[:, 4 * model_width : 4 * model_width + ff_width]
    small_part = jnp.transpose(model_summed[:, 4 * model_width + ff_width :])
    gain_part = small_part[0:2]
    shift_part = small_part[2:8]
    down_part = unit_summed[:, :model_width]
    up_shift_part = unit_summed[:, model_width]
    ends_out = jnp.where(section_first, jnp.stack(input_list), jnp.stack(top_list))[None]
    return (
        ends_out,
        qkv_part[None],
        out_part[None],
        up_part[None],
        down_part[None],
        gain_part[None],
        shift_part[None],
        up_shift_part[None],
    )


def solution(mesh):
    in_specs = (
        P("section", None, "clip", "seq", None),
        P(),
        P("section", ("clip", "seq"), None),
        P("section", ("clip", "seq"), None),
        P("section", ("clip", "seq"), None),
        P("section", ("clip", "seq"), None),
        P("section", None, ("clip", "seq")),
        P("section", None, ("clip", "seq")),
        P("section", ("clip", "seq")),
    )
    out_specs = (
        P("section", None, "clip", "seq", None),
        P("section", ("clip", "seq"), None),
        P("section", ("clip", "seq"), None),
        P("section", ("clip", "seq"), None),
        P("section", ("clip", "seq"), None),
        P("section", None, ("clip", "seq")),
        P("section", None, ("clip", "seq")),
        P("section", ("clip", "seq")),
    )
    return jax.shard_map(
        on_device, mesh=mesh, in_specs=in_specs, out_specs=out_specs, check_vma=False
    )
```

profile of v0, /device:TPU:0, one launch (start us, length us, event | category | flops | bytes accessed | tf_op | source)
XLA Modules:
  0.0 888.7 jit_solution(1871168648569397522)
XLA Ops:
  12.9 36.6 %all-reduce = bf16[3072]{0:T(1024)(128)(2,1)S(1)} all-reduce(bf16[3072]{0:T(1024)(128)(2,1)S(1)} %dynamic-update-slice), channel_id=9, replica_groups=mesh['section'=2,'clip'=4,'seq'=4] {'clip','seq'}, use_global_device_ids=true, to_apply=%add | all-reduce | flops 3072 | bytes 12288
  51.0 33.1 %all-gather.1 = bf16[1,6,768]{1,0,2:T(2,128)(2,1)S(1)} all-gather(bf16[1,6,48]{1,0,2:T(2,128)(2,1)S(1)} %copy.120), channel_id=3, replica_groups=mesh['section'=2,'clip'=4,'seq'=4] {'clip','seq'}, dimensions={2}, use_global_device_ids=true | all-gather | bytes 9792 | tf_op jit(solution)/shard_map/all_gather | solution.py:237
  84.5 34.3 %all-gather = bf16[1,2,768]{1,0,2:T(2,128)(2,1)S(1)} all-gather(bf16[1,2,48]{1,0,2:T(2,128)(2,1)S(1)} %copy.119), channel_id=2, replica_groups=mesh['section'=2,'clip'=4,'seq'=4] {'clip','seq'}, dimensions={2}, use_global_device_ids=true | all-gather | bytes 3264 | tf_op jit(solution)/shard_map/all_gather | solution.py:236
  124.2 12.8 %slice_reduce_fusion = (f32[768]{0:T(1024)S(1)}, f32[768]{0:T(1024)S(1)}, f32[768]{0:T(1024)S(1)}, f32[768]{0:T(1024)S(1)}, f32[768]{0:T(1024)S(1)}, /*index=5*/f32[768]{0:T(1024)S(1)}) fusion(f32[1,6,768]{1,0,2:T(1,128)S(1)} %convert_element_type.551), kind=kLoop, calls=%fused_computation.298 | loop fusion | bytes 36864 | tf_op jit(solution)/shard_map/slice | solution.py:95
  140.0 18.0 %all-gather.4 = bf16[256,768]{1,0:T(8,128)(2,1)S(1)} all-gather(bf16[64,768]{1,0:T(8,128)(2,1)S(1)} %slice.241), channel_id=6, replica_groups=mesh['section'=2,'clip'=4,'seq'=4] {'seq'}, dimensions={0}, use_global_device_ids=true | all-gather | bytes 491520 | tf_op jit(solution)/shard_map/all_gather | solution.py:74
  158.2 14.4 %all-gather.3 = bf16[256,768]{1,0:T(8,128)(2,1)S(1)} all-gather(bf16[64,768]{1,0:T(8,128)(2,1)S(1)} %get-tuple-element.109), channel_id=5, replica_groups=mesh['section'=2,'clip'=4,'seq'=4] {'seq'}, dimensions={0}, use_global_device_ids=true | all-gather | bytes 491520 | tf_op jit(solution)/shard_map/all_gather | solution.py:77
  175.9 5.6 fusion.131
  181.6 35.8 %all-gather.24.cloned.1.call-done = bf16[1,3072,768]{2,1,0:T(8,128)(2,1)} async-done(((bf16[1,192,768]{2,1,0:T(8,128)(2,1)}), bf16[1,3072,768]{2,1,0:T(8,128)(2,1)}) %all-gather.24.cloned.1.call-update) | async-done | bytes 4718608 | tf_op jit(solution)/shard_map/all_gather | solution.py:235
  229.5 15.2 %all-gather.9 = bf16[256,768]{1,0:T(8,128)(2,1)S(1)} all-gather(bf16[64,768]{1,0:T(8,128)(2,1)S(1)} %get-tuple-element.107), channel_id=11, replica_groups=mesh['section'=2,'clip'=4,'seq'=4] {'seq'}, dimensions={0}, use_global_device_ids=true | all-gather | bytes 491520 | tf_op jit(solution)/shard_map/all_gather | solution.py:77
  244.7 14.2 %all-gather.10 = bf16[256,768]{1,0:T(8,128)(2,1)S(1)} all-gather(bf16[64,768]{1,0:T(8,128)(2,1)S(1)} %slice.240), channel_id=12, replica_groups=mesh['section'=2,'clip'=4,'seq'=4] {'seq'}, dimensions={0}, use_global_device_ids=true | all-gather | bytes 491520 | tf_op jit(solution)/shard_map/all_gather | solution.py:74
  265.5 6.1 fusion.134
  288.2 15.8 %all-gather.11 = bf16[256,768]{1,0:T(8,128)(2,1)} all-gather(bf16[64,768]{1,0:T(8,128)(2,1)S(1)} %copy-done.98), channel_id=13, replica_groups=mesh['section'=2,'clip'=4,'seq'=4] {'seq'}, dimensions={0}, use_global_device_ids=true | all-gather | bytes 491520 | tf_op jit(solution)/shard_map/all_gather | solution.py:77
  304.0 14.6 %all-gather.12 = bf16[256,768]{1,0:T(8,128)(2,1)S(1)} all-gather(bf16[64,768]{1,0:T(8,128)(2,1)S(1)} %copy-done.99), channel_id=14, replica_groups=mesh['section'=2,'clip'=4,'seq'=4] {'seq'}, dimensions={0}, use_global_device_ids=true | all-gather | bytes 491520 | tf_op jit(solution)/shard_map/all_gather | solution.py:74
  333.2 5.9 fusion.152
  367.1 10.1 %reduce-scatter.27.cloned.1.call-done = bf16[64,768]{1,0:T(8,128)(2,1)} async-done(((bf16[256,768]{1,0:T(8,128)(2,1)}), bf16[64,768]{1,0:T(8,128)(2,1)}) %reduce-scatter.27.cloned.1.call-update) | async-done | bytes 98320
  378.5 19.9 %reduce-scatter.25.cloned.1.call-done = bf16[64,768]{1,0:T(8,128)(2,1)} async-done(((bf16[256,768]{1,0:T(8,128)(2,1)}), bf16[64,768]{1,0:T(8,128)(2,1)}) %reduce-scatter.25.cloned.1.call-update) | async-done | bytes 98320
  414.3 5.3 fusion.144
  446.1 7.7 reduce-scatter.31.cloned.1.call-done
  455.1 20.6 %reduce-scatter.29.cloned.1.call-done = bf16[64,768]{1,0:T(8,128)(2,1)} async-done(((bf16[256,768]{1,0:T(8,128)(2,1)}), bf16[64,768]{1,0:T(8,128)(2,1)}) %reduce-scatter.29.cloned.1.call-update) | async-done | bytes 98320
  515.7 10.8 %copy.173 = f32[3072,769]{1,0:T(8,128)} copy(f32[3072,769]{0,1:T(8,128)} %pad_maximum_fusion) | data formatting | bytes 18898944
  560.4 6.7 fusion.265
  567.1 23.1 %concatenate.70 = f32[768,6152]{1,0:T(8,128)} concatenate(f32[768,2304]{1,0:T(8,128)} %fusion.265, f32[768,768]{1,0:T(8,128)S(1)} %copy-done.3, f32[768,3072]{1,0:T(8,128)} %fusion.252, f32[768,1]{1,0:T(8,128)} %reduce_sum.696, f32[768,1]{1,0:T(8,128)} %reduce_sum.697, f32[768,1]{1,0:T(8,128)} %reduce_sum.698, f32[768,1]{1,0:T(8,128)S(1)} %copy-done.54, f32[768,1]{1,0:T(8,128)} %stack.187, ...), dimensions={1} | concatenate | bytes 37797888 | tf_op jit(solution)/shard_map/concatenate | solution.py:321
  596.6 74.6 %reduce-scatter.37.cloned.1.call-done = f32[192,769]{1,0:T(8,128)} async-done(((f32[3072,769]{1,0:T(8,128)}), f32[192,769]{1,0:T(8,128)}) %reduce-scatter.37.cloned.1.call-update) | async-done | bytes 590608
  675.2 198.8 %reduce-scatter.23.cloned.1.call-done = f32[48,6152]{1,0:T(8,128)} async-done(((f32[768,6152]{1,0:T(8,128)}), f32[48,6152]{1,0:T(8,128)}) %reduce-scatter.23.cloned.1.call-update) | async-done | bytes 1181200 | tf_op jit(solution)/shard_map/reduce_scatter | solution.py:320
  (597 shorter events, 229.7 us)
Async XLA Ops:
  7.2 112.1 %copy-start.36 = (bf16[1,2,1,64,768]{4,3,2,1,0:T(8,128)(2,1)S(1)}, bf16[1,2,1,64,768]{4,3,2,1,0:T(8,128)(2,1)}, u32[]{:S(2)}) copy-start(bf16[1,2,1,64,768]{4,3,2,1,0:T(8,128)(2,1)} %param.9) | copy-start | bytes 589828
  7.2 129.8 %all-gather.18.cloned.1.call-start = ((), (), s32[]{:S(2)}) async-start(), calls=%async_computation.9 | async-start | bytes 3760128 | tf_op jit(solution)/shard_map/all_gather | solution.py:232
  7.9 165.9 %all-gather.20.cloned.1.call-start = ((), (), s32[]{:S(2)}) async-start(), calls=%async_computation.10 | async-start | bytes 1253376 | tf_op jit(solution)/shard_map/all_gather | solution.py:233
  8.7 167.2 %all-gather.22.cloned.1.call-start = ((), (), s32[]{:S(2)}) async-start(), calls=%async_computation.11 | async-start | bytes 5013504 | tf_op jit(solution)/shard_map/all_gather | solution.py:234
  9.4 208.0 %all-gather.24.cloned.1.call-start = ((), (), s32[]{:S(2)}) async-start(), calls=%async_computation.12 | async-start | bytes 5013504 | tf_op jit(solution)/shard_map/all_gather | solution.py:235
  10.0 367.3 %reduce-scatter.27.cloned.1.call-start = ((), (), s32[]{:S(2)}) async-start(), calls=%async_computation.14 | async-start | bytes 491520
  49.5 215.9 %copy-start.123 = (f32[3072]{0:T(1024)}, f32[3072]{0:T(1024)S(1)}, u32[]{:S(2)}) copy-start(f32[3072]{0:T(1024)S(1)} %convert_element_type.553) | copy-start | bytes 36868
  136.9 127.8 %copy-start.112 = (f32[768]{0:T(1024)}, f32[768]{0:T(1024)S(1)}, u32[]{:S(2)}) copy-start(f32[768]{0:T(1024)S(1)} %get-tuple-element.59) | copy-start | bytes 9220
  137.0 128.5 %copy-start.115 = (f32[768]{0:T(1024)}, f32[768]{0:T(1024)S(1)}, u32[]{:S(2)}) copy-start(f32[768]{0:T(1024)S(1)} %get-tuple-element.58) | copy-start | bytes 9220
  175.6 157.0 %copy-start.8 = (f32[64,768]{1,0:T(8,128)}, f32[64,768]{1,0:T(8,128)S(1)}, u32[]{:S(2)}) copy-start(f32[64,768]{1,0:T(8,128)S(1)} %get-tuple-element.141) | copy-start | bytes 589828
  220.8 5.8 collective-permute-start
  227.5 56.9 %copy-start.15 = (bf16[1,64,768]{2,1,0:T(8,128)(2,1)}, bf16[1,64,768]{2,1,0:T(8,128)(2,1)S(1)}, u32[]{:S(2)}) copy-start(bf16[1,64,768]{2,1,0:T(8,128)(2,1)S(1)} %get-tuple-element.91) | copy-start | bytes 294916
  273.3 6.6 collective-permute-start.1
  278.4 66.0 %copy-start.57 = (bf16[64,768]{1,0:T(8,128)(2,1)}, bf16[64,768]{1,0:T(8,128)(2,1)S(1)}, u32[]{:S(2)}) copy-start(bf16[64,768]{1,0:T(8,128)(2,1)S(1)} %get-tuple-element.121) | copy-start | bytes 294916
  332.4 164.3 %copy-start.6 = (f32[64,768]{1,0:T(8,128)}, f32[64,768]{1,0:T(8,128)S(1)}, u32[]{:S(2)}) copy-start(f32[64,768]{1,0:T(8,128)S(1)} %get-tuple-element.153) | copy-start | bytes 589828
  356.2 42.2 %reduce-scatter.25.cloned.1.call-start = ((), (), s32[]{:S(2)}) async-start(), calls=%async_computation.13 | async-start | bytes 491520
  365.9 87.9 %reduce-scatter.31.cloned.1.call-start = ((), (), s32[]{:S(2)}) async-start(), calls=%async_computation.16 | async-start | bytes 491520
  404.6 9.7 %collective-permute-start.2 = (bf16[1,64,768]{2,1,0:T(8,128)(2,1)}, bf16[1,64,768]{2,1,0:T(8,128)(2,1)S(1)}, u32[]{:S(2)}, u32[]{:S(2)}) collective-permute-start(bf16[1,64,768]{2,1,0:T(8,128)(2,1)} %fusion.360), channel_id=1, source_target_pairs={{16,0},{17,1},{18,2},{19,3},{20,4},{21,5},{22,6},{23,7},{24,8},{25... | collective-permute-start | bytes 294920 | tf_op jit(solution)/shard_map/ppermute | solution.py:12
  433.7 42.0 %reduce-scatter.29.cloned.1.call-start = ((), (), s32[]{:S(2)}) async-start(), calls=%async_computation.15 | async-start | bytes 491520
  445.1 96.0 %reduce-scatter.35.cloned.1.call-start = ((), (), s32[]{:S(2)}) async-start(), calls=%async_computation.18 | async-start | bytes 491520
  482.0 6.5 collective-permute-start.3
  506.3 39.8 %reduce-scatter.33.cloned.1.call-start = ((), (), s32[]{:S(2)}) async-start(), calls=%async_computation.17 | async-start | bytes 491520
  509.5 161.7 %reduce-scatter.37.cloned.1.call-start = ((), (), s32[]{:S(2)}) async-start(), calls=%async_computation.19 | async-start | bytes 11698176
  526.6 347.3 %reduce-scatter.23.cloned.1.call-start = ((), (), s32[]{:S(2)}) async-start(), calls=%async_computation.8 | async-start | bytes 20471808 | tf_op jit(solution)/shard_map/reduce_scatter | solution.py:320
  (157 other events, 1025.1 us)
Sparse Core Ops, SparseCore 0:
  10.3 52.0 all-gather.17
  64.7 38.1 all-gather.19
  105.2 57.0 all-gather.21
  164.4 52.9 all-gather.23
  356.3 20.8 reduce-scatter.26
  379.5 18.8 reduce-scatter.24
  433.8 20.0 reduce-scatter.30
  456.8 18.8 reduce-scatter.28
  506.4 17.9 reduce-scatter.34
  527.2 18.8 reduce-scatter.32
  550.2 120.9 reduce-scatter.36
  675.8 198.1 reduce-scatter.22
where the time goes:
time: 900 us; the launch traced here: 889 us
  waiting for transfers between devices  379 us (42%)
  blocking collectives  196 us (22%)
  local copies, waits for them, and re-layouts  144 us (16%)
  matrix products  107 us (12%)
  other arithmetic  32.2 us (4%)
  between operations  19.1 us (2%)
  starting transfers between devices  11.5 us (1%)
    reduce_scatter x1, waiting for transfers between devices, on_device(): lax.psum_scatter(jnp.concatenate([transposed_times(first_left, joined[1])...  199 us
    unnamed x19, waiting for transfers between devices  137 us
    unnamed x364, local copies, waits for them, and re-layouts  61.4 us
    all_gather x3, blocking collectives, layer_forward(): lax.all_gather(key_rows.reshape(clip_count, frames, model_width), 'seq',...  46.8 us
    all_gather x3, blocking collectives, layer_forward(): lax.all_gather(value_rows.reshape(clip_count, frames, model_width), 'seq'...  45.4 us
    unnamed x1, blocking collectives  36.6 us
    all_gather x1, waiting for transfers between devices, on_device(): lax.all_gather(local_shards[3], ('clip', 'seq'), axis=0, tiled=True)  35.8 us
    dot_general x12, matrix products, matmul(): return jnp.dot(left, right, preferred_element_type=jnp.float32)  34.4 us
  transfers between devices with their start and end apart: 16, of which 11 were waited for; matrix products, arithmetic and copies ran while one was open for 18% of the time, Pallas kernels for 0%

commit v1 on v0

v1 whole, which is shorter than its diff:
```python
import jax
import jax.numpy as jnp
from jax import lax
from jax.sharding import Mesh
from jax.sharding import PartitionSpec as P

HEAD_DIM = 64
SCALE = HEAD_DIM ** (-0.5)


def norm_parts(values):
    centered = values - jnp.mean(values, axis=-1, keepdims=True)
    inverse = lax.rsqrt(jnp.mean(centered * centered, axis=-1, keepdims=True) + 1e-05)
    return centered * inverse, inverse


def norm_back(grad_hat, normal, inverse):
    first_term = grad_hat - jnp.mean(grad_hat, axis=-1, keepdims=True)
    return inverse * (first_term - normal * jnp.mean(grad_hat * normal, axis=-1, keepdims=True))


def matmul(left, right):
    return jnp.dot(left, right, preferred_element_type=jnp.float32)


def times_transposed(left, right):
    return lax.dot_general(
        left, right, (((1,), (1,)), ((), ())), preferred_element_type=jnp.float32
    )


def transposed_times(left, right):
    return lax.dot_general(
        left, right, (((0,), (0,)), ((), ())), preferred_element_type=jnp.float32
    )


def product(spec, left, right):
    return jnp.einsum(spec, left, right, preferred_element_type=jnp.float32)


def to_heads(rows, groups, clips, frames):
    peers = lax.axis_size("seq")
    own = rows.shape[1] // (groups * peers)
    parts = rows.reshape(clips, frames, groups, peers, own).transpose(3, 2, 0, 1, 4)
    got = lax.all_to_all(parts, "seq", 0, 0)
    got = got.transpose(1, 2, 0, 3, 4).reshape(groups, clips, peers * frames, own)
    return got.reshape(groups, clips, peers * frames, own // HEAD_DIM, HEAD_DIM)


def from_heads(heads, groups, clips, frames):
    peers = lax.axis_size("seq")
    own = heads.shape[-1]
    parts = heads.reshape(groups, clips, peers, frames, own).transpose(2, 0, 1, 3, 4)
    got = lax.all_to_all(parts, "seq", 0, 0)
    return got.transpose(2, 3, 1, 0, 4).reshape(clips * frames, groups * peers * own)


def layer_forward(row_data, clips, frames, weights):
    qkv_weight, out_weight, up_weight, down_weight, gain_rows, shifts, up_shift = weights
    width = row_data.shape[1]
    normal_one, inverse_one = norm_parts(row_data)
    normed_one = (normal_one * gain_rows[0] + shifts[0]).astype(jnp.bfloat16)
    qkv_shift = jnp.concatenate([shifts[2], jnp.zeros_like(shifts[2]), shifts[3]])
    projected = (matmul(normed_one, qkv_weight) + qkv_shift).astype(jnp.bfloat16)
    triple = to_heads(projected, 3, clips, frames)
    scores = product("nqhd,nkhd->nhqk", triple[0], triple[1]) * SCALE
    weights_exp = jnp.exp(scores - jnp.max(scores, axis=-1, keepdims=True))
    soft = weights_exp / jnp.sum(weights_exp, axis=-1, keepdims=True)
    probs = soft.astype(jnp.bfloat16)
    mixed_heads = product("nhqk,nkhd->nqhd", probs, triple[2]).astype(jnp.bfloat16)
    total = mixed_heads.shape[1]
    mixed_rows = from_heads(mixed_heads.reshape(1, clips, total, -1), 1, clips, frames)
    hidden = row_data + matmul(mixed_rows, out_weight) + shifts[4]
    normal_two, inverse_two = norm_parts(hidden)
    normed_two = (normal_two * gain_rows[1] + shifts[1]).astype(jnp.bfloat16)
    before = matmul(normed_two, up_weight) + up_shift
    half = 0.5 * (1.0 + lax.erf(before * (0.5**0.5)))
    activated = (before * half).astype(jnp.bfloat16)
    slope = half + before * jnp.exp(-0.5 * before * before) * 0.3989422804014327
    result = hidden + matmul(activated, down_weight) + shifts[5]
    kept = (
        normal_one,
        inverse_one,
        normed_one,
        triple,
        soft,
        probs,
        mixed_rows,
        normal_two,
        inverse_two,
        normed_two,
        slope,
        activated,
    )
    return result, kept


def layer_backward(grad_rows, clips, frames, kept, weights):
    qkv_weight, out_weight, up_weight, down_weight, gain_rows, shifts, up_shift = weights
    (
        normal_one,
        inverse_one,
        normed_one,
        triple,
        soft,
        probs,
        mixed_rows,
        normal_two,
        inverse_two,
        normed_two,
        slope,
        activated,
    ) = kept
    down_g = grad_rows.astype(jnp.bfloat16)
    up_g = (times_transposed(down_g, down_weight) * slope).astype(jnp.bfloat16)
    norm_two_g = times_transposed(up_g, up_weight)
    hidden_g = grad_rows + norm_back(norm_two_g * gain_rows[1], normal_two, inverse_two)
    branch_g = hidden_g.astype(jnp.bfloat16)
    mixed_g = times_transposed(branch_g, out_weight).astype(jnp.bfloat16)
    mixed_heads = to_heads(mixed_g, 1, clips, frames)[0]
    probs_g = product("nqhd,nkhd->nhqk", mixed_heads, triple[2])
    delta = jnp.sum(soft * probs_g, axis=-1, keepdims=True)
    scores_g = (soft * (probs_g - delta)).astype(jnp.bfloat16)
    query_g = product("nhqk,nkhd->nqhd", scores_g, triple[1]) * SCALE
    key_g = product("nhqk,nqhd->nkhd", scores_g, triple[0]) * SCALE
    value_g = product("nhqk,nqhd->nkhd", probs, mixed_heads)
    stacked = jnp.stack([query_g, key_g, value_g]).astype(jnp.bfloat16)
    total = stacked.shape[2]
    qkv_g = from_heads(stacked.reshape(3, clips, total, -1), 3, clips, frames)
    norm_one_g = times_transposed(qkv_g, qkv_weight)
    input_g = hidden_g + norm_back(norm_one_g * gain_rows[0], normal_one, inverse_one)
    operands = (normed_one, qkv_g, mixed_rows, branch_g, normed_two, up_g, activated, down_g)
    sums = [
        jnp.sum(norm_one_g * normal_one, axis=0),
        jnp.sum(norm_two_g * normal_two, axis=0),
        jnp.sum(norm_one_g, axis=0),
        jnp.sum(norm_two_g, axis=0),
    ]
    return input_g, operands, sums


def gather(shard):
    pairs = lax.axis_size("pair")
    own = lax.all_gather(shard, ("pair", "seq"), axis=0, tiled=True)
    own = own.reshape(pairs, own.shape[0] // pairs, own.shape[1])
    both = lax.all_gather(own, "core", axis=1, tiled=False)
    return both.reshape(-1, shard.shape[1])


def my_half(columns):
    pairs = lax.axis_size("pair")
    rows, width = columns.shape
    view = columns.reshape(rows, pairs, 2, width // (2 * pairs))
    mine = lax.dynamic_index_in_dim(view, lax.axis_index("core"), 2, keepdims=False)
    return mine.reshape(rows, width // 2)


def on_device(
    ends_in, clip_counts, qkv_weight, out_weight, up_weight, down_weight, norm_gains, vec_bias, up_bias
):
    ends_local = ends_in[0]
    batches, local_clips, frames, width = ends_local.shape
    clips = batches * local_clips
    rows = clips * frames
    owners = lax.axis_size("pair") * 2 * lax.axis_size("seq")
    share = width // owners
    ff_share = up_bias.shape[1]
    small = jnp.concatenate([norm_gains[0], vec_bias[0]], axis=0).reshape(-1)
    small = jnp.concatenate([small, up_bias[0]])
    extra = -(-small.shape[0] // width)
    extra_rows = -(-extra // 16) * 16
    small = jnp.pad(small, (0, extra_rows * width - small.shape[0])).reshape(extra_rows, width)
    out_small = gather(jnp.concatenate([out_weight[0], small], axis=0))
    out_small = out_small.reshape(owners, share + extra_rows, width)
    out_full = out_small[:, :share].reshape(width, width)
    small_full = out_small[:, share:].reshape(owners, extra_rows * width).astype(jnp.float32)
    rows8 = small_full[:, : 8 * share].reshape(owners, 8, share)
    rows8 = rows8.transpose(1, 0, 2).reshape(8, width)
    up_shift = small_full[:, 8 * share : 8 * share + ff_share].reshape(-1)
    weights = (
        gather(qkv_weight[0]),
        out_full,
        gather(up_weight[0]),
        gather(down_weight[0]),
        rows8[:2],
        rows8[2:],
        up_shift,
    )
    first = lax.axis_index("section") == 0
    ends_rows = ends_local.reshape(rows, width)
    passed, _ = layer_forward(ends_rows.astype(jnp.float32), clips, frames, weights)
    link = lax.ppermute(passed.astype(jnp.bfloat16), "section", [(0, 1)])
    layer_in = jnp.where(first, ends_rows, link).astype(jnp.float32)
    top, kept = layer_forward(layer_in, clips, frames, weights)

    clip_ids = (lax.axis_index("pair") * 2 + lax.axis_index("core")) * local_clips
    clip_ids = clip_ids + jnp.arange(local_clips, dtype=jnp.int32)
    valid = (clip_ids[None, :] < clip_counts[:, None]).astype(jnp.bfloat16)
    cotangent = (ends_local * valid[:, :, None, None]).reshape(rows, width)
    passed_g, _, _ = layer_backward(
        cotangent.astype(jnp.float32), clips, frames, kept, weights
    )
    link_g = lax.ppermute(passed_g.astype(jnp.bfloat16), "section", [(1, 0)])
    grad_in = jnp.where(first, link_g, cotangent).astype(jnp.float32)
    bottom, operands, sums = layer_backward(grad_in, clips, frames, kept, weights)

    def over_rows(index):
        return jnp.sum(operands[index], axis=0, dtype=jnp.float32)

    qkv_sum = over_rows(1)
    columns = jnp.stack(
        sums + [qkv_sum[:width], qkv_sum[2 * width :], over_rows(3), over_rows(7)]
    )
    small_g = jnp.concatenate(
        [
            columns.reshape(8, owners, share).transpose(1, 0, 2).reshape(owners, 8 * share),
            over_rows(5).reshape(owners, ff_share),
        ],
        axis=1,
    )
    spare = extra_rows * width - small_g.shape[1]
    small_g = jnp.pad(small_g, ((0, 0), (0, spare))).reshape(owners * extra_rows, width)
    small_half = lax.psum_scatter(
        small_g.reshape(lax.axis_size("pair"), 2, -1, width),
        "core",
        scatter_dimension=1,
        tiled=False,
    ).reshape(owners // 2, extra_rows, width)

    def share_grad(left, right, more=None):
        both_left = lax.all_gather(left, "core", axis=0, tiled=True)
        both_right = lax.all_gather(right, "core", axis=0, tiled=True)
        part = transposed_times(my_half(both_left), both_right).astype(jnp.bfloat16)
        if more is not None:
            part = part.reshape(owners // 2, -1, part.shape[1])
            part = jnp.concatenate([part, more.astype(jnp.bfloat16)], axis=1)
            part = part.reshape(-1, part.shape[2])
        return lax.psum_scatter(
            part, ("pair", "seq"), scatter_dimension=0, tiled=True
        ).astype(jnp.float32)

    down_part = share_grad(operands[6], operands[7])
    up_part = share_grad(operands[4], operands[5])
    out_part = share_grad(operands[2], operands[3], small_half)
    qkv_part = share_grad(operands[0], operands[1])
    small_part = out_part[share:].reshape(-1)
    rows_part = small_part[: 8 * share].reshape(8, share)
    ends_out = jnp.where(first, bottom, top).reshape(1, batches, local_clips, frames, width)
    return (
        ends_out,
        qkv_part[None],
        out_part[:share][None],
        up_part[None],
        down_part[None],
        rows_part[None, :2],
        rows_part[None, 2:],
        small_part[None, 8 * share : 8 * share + ff_share],
    )


def solution(mesh):
    sections, clips, seqs = mesh.devices.shape
    fine = Mesh(
        mesh.devices.reshape(sections, clips // 2, 2, seqs), ("section", "pair", "core", "seq")
    )
    spread = ("pair", "core", "seq")
    ends = P("section", None, ("pair", "core"), "seq", None)
    rowed = P("section", spread, None)
    lanes = P("section", None, spread)
    up_bias = P("section", spread)
    return jax.shard_map(
        on_device,
        mesh=fine,
        in_specs=(ends, P(), rowed, rowed, rowed, rowed, lanes, lanes, up_bias),
        out_specs=(ends, rowed, rowed, rowed, rowed, lanes, lanes, up_bias),
        check_vma=False,
    )
```

time: 900 us -> 822 us (0.913)
  blocking collectives: 196 us -> 135 us
  waiting for transfers between devices: 379 us -> 417 us
  local copies, waits for them, and re-layouts: 144 us -> 111 us
  matrix products: 107 us -> 80.3 us
  starting transfers between devices: 11.5 us -> 21.9 us
    unnamed x19 -> x14, waiting for transfers between devices: 137 us -> 2.92 us
    all_gather x8 -> x6, blocking collectives: 160 us -> 55.1 us  [the longest x1 41 us: gather(): own = lax.all_gather(shard, ('pair', 'seq'), axis=0, tiled=True)]
    all_gather x4 -> x10, waiting for transfers between devices: 35.9 us -> 138 us  [the longest x3 116 us: gather(): own = lax.all_gather(shard, ('pair', 'seq'), axis=0, tiled=True)]
    all_to_all x0 -> x4, blocking collectives: none -> 74 us  [the longest x2 38.4 us: from_heads(): got = lax.all_to_all(parts, 'seq', 0, 0)]
    unnamed x364 -> x142, local copies, waits for them, and re-layouts: 61.4 us -> 15.1 us
    reduce_scatter x1 -> x4, waiting for transfers between devices: 199 us -> 234 us  [share_grad(): lax.psum_scatter(part, ('pair', 'seq'), scatter_dimension=0, tiled=True)]
    all_to_all x0 -> x4, waiting for transfers between devices: none -> 32.6 us  [the longest x2 23.3 us: to_heads(): got = lax.all_to_all(parts, 'seq', 0, 0)]
    unnamed x1, blocking collectives: 36.6 us -> 5.66 us
  transfers between devices with their start and end apart: 16 -> 20, of which waited for: 11 -> 15; matrix products, arithmetic and copies ran while one was open for 18% -> 12% of each run, Pallas kernels for 0% -> 0%
where the time goes in v1:
time: 822 us; the launch traced here: 811 us
  waiting for transfers between devices  417 us (51%)
  blocking collectives  135 us (16%)
  local copies, waits for them, and re-layouts  111 us (14%)
  matrix products  80.3 us (10%)
  other arithmetic  30.9 us (4%)
  starting transfers between devices  21.9 us (3%)
  between operations  15.3 us (2%)
    reduce_scatter x4, waiting for transfers between devices, share_grad(): lax.psum_scatter(part, ('pair', 'seq'), scatter_dimension=0, tiled=True)  234 us
    all_gather x3, waiting for transfers between devices, gather(): own = lax.all_gather(shard, ('pair', 'seq'), axis=0, tiled=True)  116 us
    all_gather x1, blocking collectives, gather(): own = lax.all_gather(shard, ('pair', 'seq'), axis=0, tiled=True)  41 us
    all_to_all x2, blocking collectives, from_heads(): got = lax.all_to_all(parts, 'seq', 0, 0)  38.4 us
    all_to_all x2, blocking collectives, to_heads(): got = lax.all_to_all(parts, 'seq', 0, 0)  35.7 us
    dot_general x7, matrix products, times_transposed(): lax.dot_general(left, right, (((1,), (1,)), ((), ())), preferred_element_...  28.3 us
    all_to_all x2, waiting for transfers between devices, to_heads(): got = lax.all_to_all(parts, 'seq', 0, 0)  23.3 us
    dot_general x7, matrix products, matmul(): return jnp.dot(left, right, preferred_element_type=jnp.float32)  21.7 us
  transfers between devices with their start and end apart: 20, of which 15 were waited for; matrix products, arithmetic and copies ran while one was open for 12% of the time, Pallas kernels for 0%

profile of v1, /device:TPU:0, one launch (start us, length us, event | category | flops | bytes accessed | tf_op | source)
XLA Modules:
  0.0 810.7 jit_solution(3364922580359247)
XLA Ops:
  11.9 41.0 %all_gather.48 = bf16[512,768]{1,0:T(8,128)(2,1)} all-gather(bf16[64,768]{1,0:T(8,128)(2,1)S(1)} %pad_maximum_fusion.1), channel_id=1, replica_groups=mesh['section'=2,'pair'=2,'core'=2,'seq'=4] {'pair','seq'}, dimensions={0}, use_global_device_ids=true | all-gather | bytes 884736 | tf_op jit(solution)/shard_map/all_gather | solution.py:145
  53.0 9.0 %all-gather.28.cloned.1.call-done = bf16[1,384,2304]{2,1,0:T(8,128)(2,1)} async-done(((bf16[1,48,2304]{2,1,0:T(8,128)(2,1)}), bf16[1,384,2304]{2,1,0:T(8,128)(2,1)}) %all-gather.28.cloned.1.call-update) | async-done | bytes 1769488 | tf_op jit(solution)/shard_map/all_gather | solution.py:145
  62.0 54.3 %all-gather.32.cloned.1.call-done = bf16[1,1536,768]{2,1,0:T(8,128)(2,1)} async-done(((bf16[1,192,768]{2,1,0:T(8,128)(2,1)}), bf16[1,1536,768]{2,1,0:T(8,128)(2,1)}) %all-gather.32.cloned.1.call-update) | async-done | bytes 2359312 | tf_op jit(solution)/shard_map/all_gather | solution.py:145
  116.4 52.7 %all-gather.30.cloned.1.call-done = bf16[1,384,3072]{2,1,0:T(8,128)(2,1)} async-done(((bf16[1,48,3072]{2,1,0:T(8,128)(2,1)}), bf16[1,384,3072]{2,1,0:T(8,128)(2,1)}) %all-gather.30.cloned.1.call-update) | async-done | bytes 2359312 | tf_op jit(solution)/shard_map/all_gather | solution.py:145
  169.5 9.4 %all-gather.14.cloned.1.call-done = bf16[2,2,256,768]{3,2,1,0:T(8,128)(2,1)} async-done(((bf16[2,1,256,768]{3,2,1,0:T(8,128)(2,1)}), bf16[2,2,256,768]{3,2,1,0:T(8,128)(2,1)}) %all-gather.14.cloned.1.call-update) | async-done | bytes 1572880 | tf_op jit(solution)/shard_map/all_gather | solution.py:147
  182.1 12.1 %all-gather.16.cloned.1.call-done = bf16[2,2,192,2304]{3,2,1,0:T(8,128)(2,1)} async-done(((bf16[2,1,192,2304]{3,2,1,0:T(8,128)(2,1)}), bf16[2,2,192,2304]{3,2,1,0:T(8,128)(2,1)}) %all-gather.16.cloned.1.call-update) | async-done | bytes 3538960 | tf_op jit(solution)/shard_map/all_gather | solution.py:147
  197.7 25.2 %all_to_all.40 = bf16[4,3,2,64,192]{4,3,2,1,0:T(8,128)(2,1)S(1)} all-to-all(bf16[4,3,2,64,192]{4,3,2,1,0:T(8,128)(2,1)S(1)} %bitcast.235), channel_id=1, replica_groups=mesh['section'=2,'pair'=2,'core'=2,'seq'=4] {'seq'}, dimensions={0} | all-to-all | bytes 1179648 | tf_op jit(solution)/shard_map/all_to_all | solution.py:46
  233.8 4.9 all-to-all-done.1
  241.0 6.5 fusion.18
  269.1 17.3 %all-to-all-done.2 = bf16[4,3,2,64,192]{4,3,2,1,0:T(8,128)(2,1)} async-done(((bf16[4,3,2,64,192]{4,3,2,1,0:T(8,128)(2,1)}), bf16[4,3,2,64,192]{4,3,2,1,0:T(8,128)(2,1)}, u32[]{:S(2)}, u32[]{:S(2)}) %all-to-all-start.2) | async-done | bytes 589856 | tf_op jit(solution)/shard_map/all_to_all | solution.py:46
  327.7 4.9 multiply_convert_fusion
  332.7 8.7 %fusion.85 = (f32[128]{0:T(128)}, f32[128]{0:T(128)}, f32[128,768]{1,0:T(8,128)}) fusion(f32[128]{0:T(128)S(1)} %copy-done.58, f32[128,768]{1,0:T(8,128)} %copy-done.4, f32[128]{0:T(128)S(1)} %broadcast_multiply_fusion.10, f32[768]{0:T(1024)S(1)} %copy-done.38, bf16[768,3072]{1,0:T(8,128)(2,1)} %bitcast.222, bf16[128,768]{1,0:T(8,128)(2,1)} %bitcast.262, ...), kind=kOutput, calls=%fused_computation.198 | convolution fusion | flops 1212481280 | bytes 11998208 | tf_op jit(solution)/shard_map/dot_general | solution.py:27
  348.4 10.5 %all_to_all.41 = bf16[4,1,2,64,192]{4,3,2,1,0:T(8,128)(2,1)} all-to-all(bf16[4,1,2,64,192]{4,3,2,1,0:T(8,128)(2,1)S(1)} %bitcast.249), channel_id=1, replica_groups=mesh['section'=2,'pair'=2,'core'=2,'seq'=4] {'seq'}, dimensions={0} | all-to-all | bytes 393216 | tf_op jit(solution)/shard_map/all_to_all | solution.py:46
  380.5 19.2 %all_to_all.42 = bf16[4,3,2,64,192]{4,3,2,1,0:T(8,128)(2,1)S(1)} all-to-all(bf16[4,3,2,64,192]{4,3,2,1,0:T(8,128)(2,1)} %copy.108), channel_id=1, replica_groups=mesh['section'=2,'pair'=2,'core'=2,'seq'=4] {'seq'}, dimensions={0} | all-to-all | bytes 1179648 | tf_op jit(solution)/shard_map/all_to_all | solution.py:55
  408.2 6.3 collective-permute-done.1
  415.3 5.7 convert_reduce_fusion
  421.0 5.1 multiply_reduce_fusion.2
  438.0 6.0 all-to-all-done.6
  468.4 19.1 %all_to_all.43 = bf16[4,3,2,64,192]{4,3,2,1,0:T(8,128)(2,1)S(1)} all-to-all(bf16[4,3,2,64,192]{4,3,2,1,0:T(8,128)(2,1)} %copy.115), channel_id=1, replica_groups=mesh['section'=2,'pair'=2,'core'=2,'seq'=4] {'seq'}, dimensions={0} | all-to-all | bytes 1179648 | tf_op jit(solution)/shard_map/all_to_all | solution.py:55
  521.8 5.7 all-reduce.4
  559.5 30.5 %reduce-scatter.10.cloned.1.call-done = bf16[64,768]{1,0:T(8,128)(2,1)} async-done(((bf16[512,768]{1,0:T(8,128)(2,1)}), bf16[64,768]{1,0:T(8,128)(2,1)}) %reduce-scatter.10.cloned.1.call-update) | async-done | bytes 98320 | tf_op jit(solution)/shard_map/reduce_scatter | solution.py:239
  594.4 67.3 %reduce-scatter.14.cloned.1.call-done = bf16[192,768]{1,0:T(8,128)(2,1)} async-done(((bf16[1536,768]{1,0:T(8,128)(2,1)}), bf16[192,768]{1,0:T(8,128)(2,1)}) %reduce-scatter.14.cloned.1.call-update) | async-done | bytes 294928 | tf_op jit(solution)/shard_map/reduce_scatter | solution.py:239
  663.5 67.2 %reduce-scatter.8.cloned.1.call-done = bf16[48,2304]{1,0:T(8,128)(2,1)} async-done(((bf16[384,2304]{1,0:T(8,128)(2,1)}), bf16[48,2304]{1,0:T(8,128)(2,1)}) %reduce-scatter.8.cloned.1.call-update) | async-done | bytes 221200 | tf_op jit(solution)/shard_map/reduce_scatter | solution.py:239
  732.5 69.4 %reduce-scatter.12.cloned.1.call-done = bf16[48,3072]{1,0:T(8,128)(2,1)} async-done(((bf16[384,3072]{1,0:T(8,128)(2,1)}), bf16[48,3072]{1,0:T(8,128)(2,1)}) %reduce-scatter.12.cloned.1.call-update) | async-done | bytes 294928 | tf_op jit(solution)/shard_map/reduce_scatter | solution.py:239
  (358 shorter events, 237.5 us)
Async XLA Ops:
  7.2 54.8 %all-gather.28.cloned.1.call-start = ((), (), s32[]{:S(2)}) async-start(), calls=%async_computation.23 | async-start | bytes 1990656 | tf_op jit(solution)/shard_map/all_gather | solution.py:145
  7.9 108.4 %all-gather.32.cloned.1.call-start = ((), (), s32[]{:S(2)}) async-start(), calls=%async_computation.25 | async-start | bytes 2654208 | tf_op jit(solution)/shard_map/all_gather | solution.py:145
  8.7 160.5 %all-gather.30.cloned.1.call-start = ((), (), s32[]{:S(2)}) async-start(), calls=%async_computation.24 | async-start | bytes 2654208 | tf_op jit(solution)/shard_map/all_gather | solution.py:145
  9.4 169.5 %all-gather.14.cloned.1.call-start = ((), (), s32[]{:S(2)}) async-start(), calls=%async_computation.12 | async-start | bytes 2359296 | tf_op jit(solution)/shard_map/all_gather | solution.py:147
  52.9 141.3 %all-gather.16.cloned.1.call-start = ((), (), s32[]{:S(2)}) async-start(), calls=%async_computation.13 | async-start | bytes 5308416 | tf_op jit(solution)/shard_map/all_gather | solution.py:147
  62.0 179.0 %all-gather.20.cloned.1.call-start = ((), (), s32[]{:S(2)}) async-start(), calls=%async_computation.15 | async-start | bytes 7077888 | tf_op jit(solution)/shard_map/all_gather | solution.py:147
  116.4 52.8 %copy-start.10 = (bf16[1,2,1,64,768]{4,3,2,1,0:T(8,128)(2,1)S(1)}, bf16[1,2,1,64,768]{4,3,2,1,0:T(8,128)(2,1)}, u32[]{:S(2)}) copy-start(bf16[1,2,1,64,768]{4,3,2,1,0:T(8,128)(2,1)} %param.9) | copy-start | bytes 589828
  116.4 124.6 %all-gather.18.cloned.1.call-start = ((), (), s32[]{:S(2)}) async-start(), calls=%async_computation.14 | async-start | bytes 7077888 | tf_op jit(solution)/shard_map/all_gather | solution.py:147
  226.7 11.9 %all-to-all-start.1 = ((bf16[4,1,2,64,192]{4,3,2,1,0:T(8,128)(2,1)}), bf16[4,1,2,64,192]{4,3,2,1,0:T(8,128)(2,1)S(1)}, u32[]{:S(2)}, u32[]{:S(2)}) async-start(bf16[4,1,2,64,192]{4,3,2,1,0:T(8,128)(2,1)} %copy.94), calls=%async_computation.1 | async-start | bytes 524288 | tf_op jit(solution)/shard_map/all_to_all | solution.py:55
  241.0 17.2 %copy-start = (bf16[2,2,192,2304]{3,2,1,0:T(8,128)(2,1)S(1)}, bf16[2,2,192,2304]{3,2,1,0:T(8,128)(2,1)}, u32[]{:S(2)}) copy-start(bf16[2,2,192,2304]{3,2,1,0:T(8,128)(2,1)} %all-gather.16.cloned.1.call-done) | copy-start | bytes 10616836
  247.5 6.9 collective-permute-start
  264.7 21.6 %all-to-all-start.2 = ((bf16[4,3,2,64,192]{4,3,2,1,0:T(8,128)(2,1)}), bf16[4,3,2,64,192]{4,3,2,1,0:T(8,128)(2,1)}, u32[]{:S(2)}, u32[]{:S(2)}) async-start(bf16[4,3,2,64,192]{4,3,2,1,0:T(8,128)(2,1)} %bitcast.232), calls=%async_computation.2 | async-start | bytes 1572864 | tf_op jit(solution)/shard_map/all_to_all | solution.py:46
  306.0 18.5 %copy-start.41 = (f32[768]{0:T(1024)S(1)}, f32[768]{0:T(1024)}, u32[]{:S(2)}) copy-start(f32[768]{0:T(1024)} %copy-done.40) | copy-start | bytes 9220
  309.9 10.9 %all-to-all-start.3 = ((bf16[4,1,2,64,192]{4,3,2,1,0:T(8,128)(2,1)}), bf16[4,1,2,64,192]{4,3,2,1,0:T(8,128)(2,1)}, u32[]{:S(2)}, u32[]{:S(2)}) async-start(bf16[4,1,2,64,192]{4,3,2,1,0:T(8,128)(2,1)} %copy.101), calls=%async_computation.3 | async-start | bytes 524288 | tf_op jit(solution)/shard_map/all_to_all | solution.py:55
  345.5 17.3 %copy-start.44 = (f32[2,3,256]{2,1,0:T(4,128)S(1)}, f32[2,3,256]{2,1,0:T(4,128)}, u32[]{:S(2)}) copy-start(f32[2,3,256]{2,1,0:T(4,128)} %copy-done.43) | copy-start | bytes 18436
  406.8 7.7 collective-permute-start.1
  433.1 10.9 %all-to-all-start.6 = ((bf16[4,1,2,64,192]{4,3,2,1,0:T(8,128)(2,1)}), bf16[4,1,2,64,192]{4,3,2,1,0:T(8,128)(2,1)}, u32[]{:S(2)}, u32[]{:S(2)}) async-start(bf16[4,1,2,64,192]{4,3,2,1,0:T(8,128)(2,1)} %bitcast.248), calls=%async_computation.6 | async-start | bytes 524288 | tf_op jit(solution)/shard_map/all_to_all | solution.py:46
  437.2 94.2 %all-gather.26.cloned.1.call-start = ((), (), s32[]{:S(2)}) async-start(), calls=%async_computation.21 | async-start | bytes 2359296 | tf_op jit(solution)/shard_map/all_gather | solution.py:232
  437.9 105.9 %all-gather.22.cloned.1.call-start = ((), (), s32[]{:S(2)}) async-start(), calls=%async_computation.16 | async-start | bytes 1769472 | tf_op jit(solution)/shard_map/all_gather | solution.py:233
  492.6 57.6 %all-gather.24.cloned.1.call-start = ((), (), s32[]{:S(2)}) async-start(), calls=%async_computation.19 | async-start | bytes 2359296 | tf_op jit(solution)/shard_map/all_gather | solution.py:233
  509.6 80.4 %reduce-scatter.10.cloned.1.call-start = ((), (), s32[]{:S(2)}) async-start(), calls=%async_computation.18 | async-start | bytes 884736 | tf_op jit(solution)/shard_map/reduce_scatter | solution.py:239
  529.2 132.5 %reduce-scatter.14.cloned.1.call-start = ((), (), s32[]{:S(2)}) async-start(), calls=%async_computation.22 | async-start | bytes 2654208 | tf_op jit(solution)/shard_map/reduce_scatter | solution.py:239
  540.6 190.1 %reduce-scatter.8.cloned.1.call-start = ((), (), s32[]{:S(2)}) async-start(), calls=%async_computation.17 | async-start | bytes 1990656 | tf_op jit(solution)/shard_map/reduce_scatter | solution.py:239
  547.0 254.9 %reduce-scatter.12.cloned.1.call-start = ((), (), s32[]{:S(2)}) async-start(), calls=%async_computation.20 | async-start | bytes 2654208 | tf_op jit(solution)/shard_map/reduce_scatter | solution.py:239
  (62 other events, 246.4 us)
Sparse Core Ops, SparseCore 0:
  10.1 51.7 all-gather.27
  64.0 52.2 all-gather.31
  118.4 50.6 all-gather.29
  170.5 8.3 all-gather.13
  180.3 13.8 all-gather.15
  195.6 15.6 all-gather.19
  212.8 15.6 all-gather.17
  439.6 10.2 all-gather.25
  492.7 7.3 all-gather.21
  509.7 7.9 all-gather.23
  529.3 60.6 reduce-scatter.9
  593.7 67.9 reduce-scatter.13
  665.6 65.1 reduce-scatter.7
  734.1 67.7 reduce-scatter.11

commit v2 on v1

--- a/solution.py
+++ b/solution.py
@@ -1,6 +1,10 @@
+import functools
+
 import jax
 import jax.numpy as jnp
 from jax import lax
+from jax.experimental import pallas as pl
+from jax.experimental.pallas import tpu as pltpu
 from jax.sharding import Mesh
 from jax.sharding import PartitionSpec as P
 
@@ -140,12 +144,265 @@
     return input_g, operands, sums
 
 
-def gather(shard):
-    pairs = lax.axis_size("pair")
-    own = lax.all_gather(shard, ("pair", "seq"), axis=0, tiled=True)
-    own = own.reshape(pairs, own.shape[0] // pairs, own.shape[1])
-    both = lax.all_gather(own, "core", axis=1, tiled=False)
-    return both.reshape(-1, shard.shape[1])
+def turn(axis, step):
+    size = lax.axis_size(axis)
+    return lax.rem(lax.axis_index(axis) + step, size)
+
+
+def offsets(size):
+    near = []
+    for step in range(1, size // 2 + 1):
+        near.append(step)
+        if size - step != step:
+            near.append(size - step)
+    return near
+
+
+def meet(partners):
+    barrier = pltpu.get_barrier_semaphore()
+    for partner in partners:
+        pl.semaphore_signal(
+            barrier, inc=1, device_id=partner, device_id_type=pl.DeviceIdType.MESH
+        )
+    pl.semaphore_wait(barrier, len(partners))
+
+
+def remote(source, target, send, receive, device):
+    return pltpu.make_async_remote_copy(
+        src_ref=source,
+        dst_ref=target,
+        send_sem=send,
+        recv_sem=receive,
+        device_id=device,
+        device_id_type=pl.DeviceIdType.MESH,
+    )
+
+
+def gather_kernel(pairs, seqs, count, *refs):
+    shards, fulls = refs[:count], refs[count : 2 * count]
+    own_sem, seq_send, pair_send, core_send, lane_recv, core_recv = refs[2 * count :]
+    pair, core, seq = (lax.axis_index(name) for name in ("pair", "core", "seq"))
+    other = {"core": 1 - core}
+    seq_steps, pair_steps = offsets(seqs), offsets(pairs)
+    meet(
+        [{"seq": turn("seq", step)} for step in seq_steps]
+        + [{"pair": turn("pair", step)} for step in pair_steps]
+        + [other]
+    )
+
+    def slot(pair_index, core_index, seq_index):
+        return (pair_index * 2 + core_index) * seqs + seq_index
+
+    started, waits = [], []
+
+    def start(copy):
+        copy.start()
+        started.append(copy)
+
+    def to_core(w, source, place, index):
+        start(
+            remote(
+                source, fulls[w].at[place], core_send.at[w, index], core_recv.at[w, index], other
+            )
+        )
+
+    def to_pairs(w, source, place, seq_step):
+        for step in pair_steps:
+            index = step * seqs + seq_step
+            start(
+                remote(
+                    source,
+                    fulls[w].at[place],
+                    pair_send.at[w, index],
+                    lane_recv.at[w, index],
+                    {"pair": turn("pair", step)},
+                )
+            )
+
+    mine = slot(pair, core, seq)
+    local = []
+    for w in range(count):
+        for step in seq_steps:
+            start(
+                remote(
+                    shards[w],
+                    fulls[w].at[mine],
+                    seq_send.at[w, step],
+                    lane_recv.at[w, step],
+                    {"seq": turn("seq", step)},
+                )
+            )
+        to_pairs(w, shards[w], mine, 0)
+        to_core(w, shards[w], mine, 0)
+        copy = pltpu.make_async_copy(shards[w], fulls[w].at[mine], own_sem.at[w])
+        copy.start()
+        local.append(copy)
+
+    def arrived(w, place, index, semaphores):
+        there = fulls[w].at[place]
+        remote(there, there, core_send.at[w, index], semaphores.at[w, index], other).wait_recv()
+
+    for w in range(count):
+        for step in seq_steps:
+            place = slot(pair, core, turn("seq", seqs - step))
+            arrived(w, place, step, lane_recv)
+            to_pairs(w, fulls[w].at[place], place, step)
+            to_core(w, fulls[w].at[place], place, step)
+        for seq_step in [0] + seq_steps:
+            for step in pair_steps:
+                place = slot(
+                    turn("pair", pairs - step), core, turn("seq", seqs - seq_step)
+                )
+                index = step * seqs + seq_step
+                arrived(w, place, index, lane_recv)
+                to_core(w, fulls[w].at[place], place, index)
+    for w in range(count):
+        for seq_step in range(seqs):
+            for step in range(pairs):
+                place = slot(
+                    turn("pair", pairs - step), 1 - core, turn("seq", seqs - seq_step)
+                )
+                arrived(w, place, step * seqs + seq_step, core_recv)
+    for copy in started:
+        copy.wait_send()
+    for copy in local:
+        copy.wait()
+
+
+def gather_all(shards):
+    pairs, seqs = lax.axis_size("pair"), lax.axis_size("seq")
+    count, lanes = len(shards), pairs * seqs
+    dma = pltpu.SemaphoreType.DMA
+    anywhere = pl.BlockSpec(memory_space=pl.ANY)
+    return pl.pallas_call(
+        functools.partial(gather_kernel, pairs, seqs, count),
+        out_shape=[jax.ShapeDtypeStruct((2 * lanes,) + x.shape, x.dtype) for x in shards],
+        in_specs=[anywhere] * count,
+        out_specs=[anywhere] * count,
+        scratch_shapes=[
+            dma((count,)),
+            dma((count, seqs)),
+            dma((count, lanes)),
+            dma((count, lanes)),
+            dma((count, lanes)),
+            dma((count, lanes)),
+        ],
+        compiler_params=pltpu.CompilerParams(collective_id=0, has_side_effects=True),
+        name="gather_weights",
+    )(*shards)
+
+
+def swap_kernel(count, *refs):
+    sources, targets = refs[:count], refs[count : 2 * count]
+    send, receive = refs[2 * count :]
+    other = {"core": 1 - lax.axis_index("core")}
+    meet([other])
+    copies = [
+        remote(sources[i], targets[i], send.at[i], receive.at[i], other) for i in range(count)
+    ]
+    for copy in copies:
+        copy.start()
+    for copy in copies:
+        copy.wait()
+
+
+def swap_cores(arrays):
+    count = len(arrays)
+    vmem = pl.BlockSpec(memory_space=pltpu.VMEM)
+    return pl.pallas_call(
+        functools.partial(swap_kernel, count),
+        out_shape=[jax.ShapeDtypeStruct(x.shape, x.dtype) for x in arrays],
+        in_specs=[vmem] * count,
+        out_specs=[vmem] * count,
+        scratch_shapes=[pltpu.SemaphoreType.DMA((count,)), pltpu.SemaphoreType.DMA((count,))],
+        compiler_params=pltpu.CompilerParams(
+            collective_id=1, has_side_effects=True, vmem_limit_bytes=24 * 2**20
+        ),
+        name="swap_cores",
+    )(*arrays)
+
+
+def scatter_kernel(pairs, seqs, count, *refs):
+    parts, outs = refs[:count], refs[count : 2 * count]
+    pair_in = refs[2 * count : 3 * count]
+    seq_out = refs[3 * count : 4 * count]
+    seq_in = refs[4 * count : 5 * count]
+    pair_send, pair_recv, seq_send, seq_recv = refs[5 * count :]
+    pair = lax.axis_index("pair")
+    seq_steps, pair_steps = offsets(seqs), offsets(pairs)
+    meet(
+        [{"seq": turn("seq", step)} for step in seq_steps]
+        + [{"pair": turn("pair", step)} for step in pair_steps]
+    )
+    order = [(w, step) for w in range(count) for step in seq_steps + [0]]
+    to_pair, to_seq = {}, {}
+    for w, seq_step in order:
+        for step in pair_steps:
+            index = (step - 1) * seqs + seq_step
+            target = turn("pair", step)
+            copy = remote(
+                parts[w].at[target * seqs + turn("seq", seq_step)],
+                pair_in[w].at[index],
+                pair_send.at[w, index],
+                pair_recv.at[w, index],
+                {"pair": target},
+            )
+            copy.start()
+            to_pair[w, index] = copy
+    for w, seq_step in order:
+        total = parts[w][pair * seqs + turn("seq", seq_step)].astype(jnp.float32)
+        for step in pair_steps:
+            index = (step - 1) * seqs + seq_step
+            to_pair[w, index].wait_recv()
+            total = total + pair_in[w][index].astype(jnp.float32)
+        if seq_step == 0:
+            outs[w][...] = total
+        else:
+            seq_out[w][seq_step - 1] = total.astype(jnp.bfloat16)
+            copy = remote(
+                seq_out[w].at[seq_step - 1],
+                seq_in[w].at[seq_step - 1],
+                seq_send.at[w, seq_step - 1],
+                seq_recv.at[w, seq_step - 1],
+                {"seq": turn("seq", seq_step)},
+            )
+            copy.start()
+            to_seq[w, seq_step] = copy
+    for w in range(count):
+        total = outs[w][...]
+        for step in seq_steps:
+            to_seq[w, step].wait_recv()
+            total = total + seq_in[w][step - 1].astype(jnp.float32)
+        outs[w][...] = total
+    for copy in list(to_pair.values()) + list(to_seq.values()):
+        copy.wait_send()
+
+
+def scatter_all(parts):
+    pairs, seqs = lax.axis_size("pair"), lax.axis_size("seq")
+    count = len(parts)
+    vmem = pl.BlockSpec(memory_space=pltpu.VMEM)
+    dma = pltpu.SemaphoreType.DMA
+    blocks = [x.shape[1:] for x in parts]
+    from_pairs = (pairs - 1) * seqs
+    return pl.pallas_call(
+        functools.partial(scatter_kernel, pairs, seqs, count),
+        out_shape=[jax.ShapeDtypeStruct(block, jnp.float32) for block in blocks],
+        in_specs=[vmem] * count,
+        out_specs=[vmem] * count,
+        scratch_shapes=[pltpu.VMEM((from_pairs,) + block, jnp.bfloat16) for block in blocks]
+        + [pltpu.VMEM((seqs - 1,) + block, jnp.bfloat16) for block in blocks] * 2
+        + [
+            dma((count, from_pairs)),
+            dma((count, from_pairs)),
+            dma((count, seqs - 1)),
+            dma((count, seqs - 1)),
+        ],
+        compiler_params=pltpu.CompilerParams(
+            collective_id=2, has_side_effects=True, vmem_limit_bytes=40 * 2**20
+        ),
+        name="scatter_grads",
+    )(*parts)
 
 
 def my_half(columns):
@@ -171,18 +428,20 @@
     extra = -(-small.shape[0] // width)
     extra_rows = -(-extra // 16) * 16
     small = jnp.pad(small, (0, extra_rows * width - small.shape[0])).reshape(extra_rows, width)
-    out_small = gather(jnp.concatenate([out_weight[0], small], axis=0))
-    out_small = out_small.reshape(owners, share + extra_rows, width)
+    out_small = jnp.concatenate([out_weight[0], small], axis=0)
+    qkv_full, out_small, up_full, down_full = gather_all(
+        [qkv_weight[0], out_small, up_weight[0], down_weight[0]]
+    )
     out_full = out_small[:, :share].reshape(width, width)
     small_full = out_small[:, share:].reshape(owners, extra_rows * width).astype(jnp.float32)
     rows8 = small_full[:, : 8 * share].reshape(owners, 8, share)
     rows8 = rows8.transpose(1, 0, 2).reshape(8, width)
     up_shift = small_full[:, 8 * share : 8 * share + ff_share].reshape(-1)
     weights = (
-        gather(qkv_weight[0]),
+        qkv_full.reshape(width, -1),
         out_full,
-        gather(up_weight[0]),
-        gather(down_weight[0]),
+        up_full.reshape(width, -1),
+        down_full.reshape(-1, width),
         rows8[:2],
         rows8[2:],
         up_shift,
@@ -221,29 +480,24 @@
     )
     spare = extra_rows * width - small_g.shape[1]
     small_g = jnp.pad(small_g, ((0, 0), (0, spare))).reshape(owners * extra_rows, width)
-    small_half = lax.psum_scatter(
-        small_g.reshape(lax.axis_size("pair"), 2, -1, width),
-        "core",
-        scatter_dimension=1,
-        tiled=False,
+    *swapped, small_other = swap_cores(list(operands) + [small_g])
+    small_half = lax.dynamic_index_in_dim(
+        (small_g + small_other).reshape(lax.axis_size("pair"), 2, -1, width),
+        lax.axis_index("core"),
+        1,
+        keepdims=False,
     ).reshape(owners // 2, extra_rows, width)
 
-    def share_grad(left, right, more=None):
-        both_left = lax.all_gather(left, "core", axis=0, tiled=True)
-        both_right = lax.all_gather(right, "core", axis=0, tiled=True)
-        part = transposed_times(my_half(both_left), both_right).astype(jnp.bfloat16)
-        if more is not None:
-            part = part.reshape(owners // 2, -1, part.shape[1])
-            part = jnp.concatenate([part, more.astype(jnp.bfloat16)], axis=1)
-            part = part.reshape(-1, part.shape[2])
-        return lax.psum_scatter(
-            part, ("pair", "seq"), scatter_dimension=0, tiled=True
-        ).astype(jnp.float32)
-
-    down_part = share_grad(operands[6], operands[7])
-    up_part = share_grad(operands[4], operands[5])
-    out_part = share_grad(operands[2], operands[3], small_half)
-    qkv_part = share_grad(operands[0], operands[1])
+    def part_grad(index):
+        left = jnp.concatenate([my_half(operands[index]), my_half(swapped[index])], axis=0)
+        right = jnp.concatenate([operands[index + 1], swapped[index + 1]], axis=0)
+        part = transposed_times(left, right).astype(jnp.bfloat16)
+        return part.reshape(owners // 2, -1, part.shape[1])
+
+    out_half = jnp.concatenate([part_grad(2), small_half.astype(jnp.bfloat16)], axis=1)
+    qkv_part, out_part, up_part, down_part = scatter_all(
+        [part_grad(0), out_half, part_grad(4), part_grad(6)]
+    )
     small_part = out_part[share:].reshape(-1)
     rows_part = small_part[: 8 * share].reshape(8, share)
     ends_out = jnp.where(first, bottom, top).reshape(1, batches, local_clips, frames, width)

time: 822 us -> 511 us (0.62)
  waiting for transfers between devices: 417 us -> 48.7 us
  Pallas kernels: 0 us -> 201 us
  blocking collectives: 135 us -> 64.4 us
  local copies, waits for them, and re-layouts: 111 us -> 83.2 us
  matrix products: 80.3 us -> 62.2 us
  between operations: 15.3 us -> 2.29 us
  other arithmetic: 30.9 us -> 19.7 us
    reduce_scatter x4 -> x0, waiting for transfers between devices: 234 us -> none  [share_grad(): lax.psum_scatter(part, ('pair', 'seq'), scatter_dimension=0, tiled=True)]
    pallas_call x0 -> x3, Pallas kernels: none -> 201 us  [the longest x1 102 us: gather_all(): pl.pallas_call(functools.partial(gather_kernel, pairs, seqs, count), out_...]
    all_gather x10 -> x0, waiting for transfers between devices: 138 us -> none  [the longest x3 116 us: gather(): own = lax.all_gather(shard, ('pair', 'seq'), axis=0, tiled=True)]
    all_gather x6 -> x0, blocking collectives: 55.1 us -> none  [the longest x1 41 us: gather(): own = lax.all_gather(shard, ('pair', 'seq'), axis=0, tiled=True)]
    all_to_all x2 -> x1, blocking collectives: 38.4 us -> 21.1 us  [from_heads(): got = lax.all_to_all(parts, 'seq', 0, 0)]
    all_to_all x2 -> x3, waiting for transfers between devices: 9.29 us -> 21.3 us  [from_heads(): got = lax.all_to_all(parts, 'seq', 0, 0)]
    all_to_all x2 -> x3, blocking collectives: 35.7 us -> 43.3 us  [to_heads(): got = lax.all_to_all(parts, 'seq', 0, 0)]
    all_to_all x2 -> x1, waiting for transfers between devices: 23.3 us -> 17.9 us  [to_heads(): got = lax.all_to_all(parts, 'seq', 0, 0)]
  transfers between devices with their start and end apart: 20 -> 6, of which waited for: 15 -> 6; matrix products, arithmetic and copies ran while one was open for 12% -> 2% of each run, Pallas kernels for 0% -> 0%
where the time goes in v2:
time: 511 us; the launch traced here: 501 us
  Pallas kernels  201 us (39%)
  local copies, waits for them, and re-layouts  83.2 us (16%)
  blocking collectives  64.4 us (13%)
  matrix products  62.2 us (12%)
  waiting for transfers between devices  48.7 us (10%)
  starting transfers between devices  19.9 us (4%)
  other arithmetic  19.7 us (4%)
    pallas_call x1, Pallas kernels, gather_all(): pl.pallas_call(functools.partial(gather_kernel, pairs, seqs, count), out_...  102 us
    pallas_call x1, Pallas kernels, scatter_all(): pl.pallas_call(functools.partial(scatter_kernel, pairs, seqs, count), out...  91.4 us
    all_to_all x3, blocking collectives, to_heads(): got = lax.all_to_all(parts, 'seq', 0, 0)  43.3 us
    dot_general x7, matrix products, times_transposed(): lax.dot_general(left, right, (((1,), (1,)), ((), ())), preferred_element_...  25.7 us
    all_to_all x3, waiting for transfers between devices, from_heads(): got = lax.all_to_all(parts, 'seq', 0, 0)  21.3 us
    all_to_all x1, blocking collectives, from_heads(): got = lax.all_to_all(parts, 'seq', 0, 0)  21.1 us
    dot_general x7, matrix products, matmul(): return jnp.dot(left, right, preferred_element_type=jnp.float32)  20.3 us
    unnamed x177, local copies, waits for them, and re-layouts  19.6 us
  transfers between devices with their start and end apart: 6, of which 6 were waited for; matrix products, arithmetic and copies ran while one was open for 2% of the time, Pallas kernels for 0%

profile of v2, /device:TPU:0, one launch (start us, length us, event | category | flops | bytes accessed | tf_op | source)
XLA Modules:
  0.0 501.0 jit_solution(243683807797280085)
XLA Ops:
  3.7 102.2 %gather_weights.1 = (bf16[16,48,2304]{2,1,0:T(8,128)(2,1)}, bf16[16,64,768]{2,1,0:T(8,128)(2,1)}, bf16[16,48,3072]{2,1,0:T(8,128)(2,1)}, bf16[16,192,768]{2,1,0:T(8,128)(2,1)}) custom-call(bf16[48,2304]{1,0:T(8,128)(2,1)} %bitcast.261, bf16[64,768]{1,0:T(8,128)(2,1)} %pad_maximum_fusion.1.refs_1_, bf16[48,3072]{1,0:T(8,128)(2,1)} %bitcast.258, ...), custom_call_target="tpu_custom_call" | custom-call | tf_op jit(solution)/shard_map/gather_weights/pallas_call | solution.py:277
  113.1 23.4 %all_to_all.40 = bf16[4,3,2,64,192]{4,3,2,1,0:T(8,128)(2,1)S(1)} all-to-all(bf16[4,3,2,64,192]{4,3,2,1,0:T(8,128)(2,1)S(1)} %bitcast.230), channel_id=1, replica_groups=mesh['section'=2,'pair'=2,'core'=2,'seq'=4] {'seq'}, dimensions={0} | all-to-all | bytes 1179648 | tf_op jit(solution)/shard_map/all_to_all | solution.py:50
  140.4 3.4 all-to-all-start.1
  146.2 6.2 %all-to-all-done.1 = bf16[4,1,2,64,192]{4,3,2,1,0:T(8,128)(2,1)S(1)} async-done(((bf16[4,1,2,64,192]{4,3,2,1,0:T(8,128)(2,1)}), bf16[4,1,2,64,192]{4,3,2,1,0:T(8,128)(2,1)S(1)}, u32[]{:S(2)}, u32[]{:S(2)}) %all-to-all-start.1) | async-done | bytes 196640 | tf_op jit(solution)/shard_map/all_to_all | solution.py:59
  153.6 5.5 %fusion.24 = bf16[128,768]{1,0:T(8,128)(2,1)S(1)} fusion(f32[128,768]{1,0:T(8,128)S(1)} %get-tuple-element.120, bf16[3072,768]{1,0:T(8,128)(2,1)} %bitcast.223, bf16[768,3072]{1,0:T(8,128)(2,1)} %bitcast.216, f32[3072]{0:T(1024)S(1)} %add.201, f32[768]{0:T(1024)S(1)} %add.206, f32[768]{0:T(1024)S(1)} %add.198, f32[768]{0:T(1024)S(1)} %mul.303, ...), kind=kOutput, calls=%fused_computation.59 | convolution fusion | flops 1211105280 | bytes 10049536 | tf_op jit(solution)/shard_map/dot_general | solution.py:27
  159.2 3.4 collective-permute-start
  170.8 3.7 all-to-all-start.2
  174.5 17.9 %all-to-all-done.2 = bf16[4,3,2,64,192]{4,3,2,1,0:T(8,128)(2,1)S(1)} async-done(((bf16[4,3,2,64,192]{4,3,2,1,0:T(8,128)(2,1)}), bf16[4,3,2,64,192]{4,3,2,1,0:T(8,128)(2,1)S(1)}, u32[]{:S(2)}, u32[]{:S(2)}) %all-to-all-start.2) | async-done | bytes 589856 | tf_op jit(solution)/shard_map/all_to_all | solution.py:50
  200.6 3.4 all-to-all-start.3
  205.5 6.6 %all-to-all-done.3 = bf16[4,1,2,64,192]{4,3,2,1,0:T(8,128)(2,1)S(1)} async-done(((bf16[4,1,2,64,192]{4,3,2,1,0:T(8,128)(2,1)}), bf16[4,1,2,64,192]{4,3,2,1,0:T(8,128)(2,1)S(1)}, u32[]{:S(2)}, u32[]{:S(2)}) %all-to-all-start.3) | async-done | bytes 196640 | tf_op jit(solution)/shard_map/all_to_all | solution.py:59
  213.4 4.6 multiply_convert_fusion
  218.0 8.1 %fusion.113 = (f32[128]{0:T(128)S(1)}, f32[128]{0:T(128)S(1)}, f32[128,768]{1,0:T(8,128)}) fusion(f32[128]{0:T(128)S(1)} %add_rsqrt_fusion.1, f32[128,768]{1,0:T(8,128)S(1)} %get-tuple-element.124, f32[128]{0:T(128)S(1)} %broadcast_multiply_fusion.10, f32[768]{0:T(1024)S(1)} %copy-done.51, bf16[768,3072]{1,0:T(8,128)(2,1)} %bitcast.218, ...), kind=kOutput, calls=%fused_computation.227 | convolution fusion | flops 1212481280 | bytes 11998208 | tf_op jit(solution)/shard_map/dot_general | solution.py:31
  229.7 10.2 %all_to_all.41 = bf16[4,1,2,64,192]{4,3,2,1,0:T(8,128)(2,1)} all-to-all(bf16[4,1,2,64,192]{4,3,2,1,0:T(8,128)(2,1)S(1)} %bitcast.240), channel_id=1, replica_groups=mesh['section'=2,'pair'=2,'core'=2,'seq'=4] {'seq'}, dimensions={0} | all-to-all | bytes 393216 | tf_op jit(solution)/shard_map/all_to_all | solution.py:50
  258.9 21.1 %all_to_all.42 = bf16[4,3,2,64,192]{4,3,2,1,0:T(8,128)(2,1)S(1)} all-to-all(bf16[4,3,2,64,192]{4,3,2,1,0:T(8,128)(2,1)} %copy.165), channel_id=1, replica_groups=mesh['section'=2,'pair'=2,'core'=2,'seq'=4] {'seq'}, dimensions={0} | all-to-all | bytes 1179648 | tf_op jit(solution)/shard_map/all_to_all | solution.py:59
  284.2 3.5 fusion.112
  289.5 6.4 %collective-permute-done.1 = bf16[128,768]{1,0:T(8,128)(2,1)S(1)} collective-permute-done((bf16[128,768]{1,0:T(8,128)(2,1)S(1)}, bf16[128,768]{1,0:T(8,128)(2,1)S(1)}, u32[]{:S(2)}, u32[]{:S(2)}) %collective-permute-start.1) | collective-permute-done | bytes 196640 | tf_op jit(solution)/shard_map/ppermute | solution.py:463
  296.7 4.7 convert_reduce_fusion
  307.8 9.7 %all_to_all.43 = bf16[4,1,2,64,192]{4,3,2,1,0:T(8,128)(2,1)S(1)} all-to-all(bf16[4,1,2,64,192]{4,3,2,1,0:T(8,128)(2,1)S(1)} %bitcast.242), channel_id=1, replica_groups=mesh['section'=2,'pair'=2,'core'=2,'seq'=4] {'seq'}, dimensions={0} | all-to-all | bytes 393216 | tf_op jit(solution)/shard_map/all_to_all | solution.py:50
  328.7 4.4 all-to-all-start.7
  341.1 8.5 %all-to-all-done.7 = bf16[4,3,2,64,192]{4,3,2,1,0:T(8,128)(2,1)} async-done(((bf16[4,3,2,64,192]{4,3,2,1,0:T(8,128)(2,1)}), bf16[4,3,2,64,192]{4,3,2,1,0:T(8,128)(2,1)}, u32[]{:S(2)}, u32[]{:S(2)}) %all-to-all-start.7) | async-done | bytes 589856 | tf_op jit(solution)/shard_map/all_to_all | solution.py:59
  354.4 4.6 fusion.62
  364.9 6.9 %swap_cores.1 = (bf16[128,768]{1,0:T(8,128)(2,1)S(1)}, bf16[128,2304]{1,0:T(8,128)(2,1)S(1)}, bf16[128,768]{1,0:T(8,128)(2,1)S(1)}, bf16[128,768]{1,0:T(8,128)(2...) custom-call(bf16[128,768]{1,0:T(8,128)(2,1)S(1)} %fusion.51.refs_0_,, ...), custom_call_target="tpu_custom_call" | custom-call | tf_op jit(solution)/shard_map/swap_cores/pallas_call | solution.py:312
  398.7 91.4 %scatter_grads.1 = (f32[48,2304]{1,0:T(8,128)S(1)}, f32[64,768]{1,0:T(8,128)S(1)}, f32[48,3072]{1,0:T(8,128)S(1)}, f32[192,768]{1,0:T(8,128)S(1)}) custom-call(bf16[8,48,2304]{2,1,0:T(8,128)(2,1)S(1)} %bitcast.204, bf16[8,64,768]{2,1,0:T(8,128)(2,1)S(1)} %pad_maximum_fusion.refs_1_, bf16[8,48,3072]{2,1,0:T(8,128)(2,1)S(1)} %bitcast.202, ...), custom_call_target="tpu_custom_call" | custom-call | tf_op jit(solution)/shard_map/scatter_grads/pallas_call | solution.py:388
  494.3 4.0 fusion.61
  (353 shorter events, 134.7 us)
Async XLA Ops:
  140.4 12.1 %all-to-all-start.1 = ((bf16[4,1,2,64,192]{4,3,2,1,0:T(8,128)(2,1)}), bf16[4,1,2,64,192]{4,3,2,1,0:T(8,128)(2,1)S(1)}, u32[]{:S(2)}, u32[]{:S(2)}) async-start(bf16[4,1,2,64,192]{4,3,2,1,0:T(8,128)(2,1)} %copy.151), calls=%async_computation.1 | async-start | bytes 524288 | tf_op jit(solution)/shard_map/all_to_all | solution.py:59
  153.6 12.5 %copy-start.57 = (f32[768]{0:T(1024)S(1)}, f32[768]{0:T(1024)}, u32[]{:S(2)}) copy-start(f32[768]{0:T(1024)} %copy-done.56) | copy-start | bytes 9220
  159.2 6.6 %collective-permute-start = (bf16[128,768]{1,0:T(8,128)(2,1)S(1)}, bf16[128,768]{1,0:T(8,128)(2,1)S(1)}, u32[]{:S(2)}, u32[]{:S(2)}) collective-permute-start(bf16[128,768]{1,0:T(8,128)(2,1)S(1)} %fusion.24), channel_id=1, source_target_pairs={{0,16},{1,17},{2,18},{3,19},{4,20},{5,21},{6,22},{7,23},{8,24},{9,... | collective-permute-start | bytes 589832 | tf_op jit(solution)/shard_map/ppermute | solution.py:452
  165.9 121.9 %copy-start.23 = (bf16[128,768]{1,0:T(8,128)(2,1)}, bf16[128,768]{1,0:T(8,128)(2,1)S(1)}, u32[]{:S(2)}) copy-start(bf16[128,768]{1,0:T(8,128)(2,1)S(1)} %get-tuple-element.108) | copy-start | bytes 589828
  170.8 21.6 %all-to-all-start.2 = ((bf16[4,3,2,64,192]{4,3,2,1,0:T(8,128)(2,1)}), bf16[4,3,2,64,192]{4,3,2,1,0:T(8,128)(2,1)S(1)}, u32[]{:S(2)}, u32[]{:S(2)}) async-start(bf16[4,3,2,64,192]{4,3,2,1,0:T(8,128)(2,1)} %bitcast.228), calls=%async_computation.2 | async-start | bytes 1572864 | tf_op jit(solution)/shard_map/all_to_all | solution.py:50
  199.4 13.1 %copy-start.55 = (f32[768]{0:T(1024)S(1)}, f32[768]{0:T(1024)}, u32[]{:S(2)}) copy-start(f32[768]{0:T(1024)} %copy-done.54) | copy-start | bytes 9220
  200.6 11.4 %all-to-all-start.3 = ((bf16[4,1,2,64,192]{4,3,2,1,0:T(8,128)(2,1)}), bf16[4,1,2,64,192]{4,3,2,1,0:T(8,128)(2,1)S(1)}, u32[]{:S(2)}, u32[]{:S(2)}) async-start(bf16[4,1,2,64,192]{4,3,2,1,0:T(8,128)(2,1)} %copy.158), calls=%async_computation.3 | async-start | bytes 524288 | tf_op jit(solution)/shard_map/all_to_all | solution.py:59
  212.9 13.1 %copy-start.20 = (f32[128,768]{1,0:T(8,128)}, f32[128,768]{1,0:T(8,128)S(1)}, u32[]{:S(2)}) copy-start(f32[128,768]{1,0:T(8,128)S(1)} %get-tuple-element.124) | copy-start | bytes 1179652
  284.2 11.8 %copy-start.77 = (bf16[128]{0:T(256)(128)(2,1)S(1)}, bf16[128]{0:T(256)(128)(2,1)}, u32[]{:S(2)}) copy-start(bf16[128]{0:T(256)(128)(2,1)} %mul.290) | copy-start | bytes 772
  287.7 9.0 %copy-start.40 = (f32[128,3072]{1,0:T(8,128)S(1)}, f32[128,3072]{1,0:T(8,128)}, u32[]{:S(2)}) copy-start(f32[128,3072]{1,0:T(8,128)} %get-tuple-element.134) | copy-start | bytes 4718596
  287.8 13.7 %slice-start = ((s8[4718592]{0:T(1024)(128)(4,1)}), s8[4194304]{0:T(1024)(128)(4,1)S(1)}, s32[]{:S(2)}) async-start(s8[4718592]{0:T(1024)(128)(4,1)} %bitcast.219), calls=%async_computation.8 | async-start | bytes 8388608
  288.0 8.0 %collective-permute-start.1 = (bf16[128,768]{1,0:T(8,128)(2,1)S(1)}, bf16[128,768]{1,0:T(8,128)(2,1)S(1)}, u32[]{:S(2)}, u32[]{:S(2)}) collective-permute-start(bf16[128,768]{1,0:T(8,128)(2,1)S(1)} %fusion.56), channel_id=1, source_target_pairs={{16,0},{17,1},{18,2},{19,3},{20,4},{21,5},{22,6},{23,7},{24,8},{25... | collective-permute-start | bytes 589832 | tf_op jit(solution)/shard_map/ppermute | solution.py:463
  305.3 12.4 %copy-start.2 = (bf16[128,768]{1,0:T(8,128)(2,1)}, bf16[128,768]{1,0:T(8,128)(2,1)S(1)}, u32[]{:S(2)}) copy-start(bf16[128,768]{1,0:T(8,128)(2,1)S(1)} %get-tuple-element.105.refs_3_) | copy-start | bytes 589828
  306.5 11.5 %copy-start.47 = (bf16[2,256,3,64]{1,3,2,0:T(8,128)(2,1)S(1)}, bf16[2,256,3,64]{1,3,2,0:T(8,128)(2,1)}, u32[]{:S(2)}) copy-start(bf16[2,256,3,64]{1,3,2,0:T(8,128)(2,1)} %copy-done.46) | copy-start | bytes 589828
  328.7 21.0 %all-to-all-start.7 = ((bf16[4,3,2,64,192]{4,3,2,1,0:T(8,128)(2,1)}), bf16[4,3,2,64,192]{4,3,2,1,0:T(8,128)(2,1)}, u32[]{:S(2)}, u32[]{:S(2)}) async-start(bf16[4,3,2,64,192]{4,3,2,1,0:T(8,128)(2,1)} %copy.172), calls=%async_computation.7 | async-start | bytes 1572864 | tf_op jit(solution)/shard_map/all_to_all | solution.py:59
  340.1 14.3 %copy-start.24 = (bf16[128,768]{1,0:T(8,128)(2,1)S(1)}, bf16[128,768]{1,0:T(8,128)(2,1)}, u32[]{:S(2)}) copy-start(bf16[128,768]{1,0:T(8,128)(2,1)} %copy-done.23) | copy-start | bytes 589828
  340.1 14.3 %copy-start.60 = (f32[128]{0:T(128)S(1)}, f32[128]{0:T(128)}, u32[]{:S(2)}) copy-start(f32[128]{0:T(128)} %copy-done.58) | copy-start | bytes 1540
  340.1 14.3 %copy-start.73 = (f32[128]{0:T(128)S(1)}, f32[128]{0:T(128)}, u32[]{:S(2)}) copy-start(f32[128]{0:T(128)} %copy-done.71) | copy-start | bytes 1540
  382.0 8.4 %copy-start.14 = (bf16[128,768]{1,0:T(8,128)(2,1)S(1)}, bf16[128,768]{1,0:T(8,128)(2,1)}, u32[]{:S(2)}) copy-start(bf16[128,768]{1,0:T(8,128)(2,1)} %copy-done.13) | copy-start | bytes 589828
  398.7 95.6 %copy-start.78 = (f32[128]{0:T(128)S(1)}, f32[128]{0:T(128)}, u32[]{:S(2)}) copy-start(f32[128]{0:T(128)} %get-tuple-element.85) | copy-start | bytes 1540
  398.7 95.6 %copy-start.22 = (f32[128,768]{1,0:T(8,128)S(1)}, f32[128,768]{1,0:T(8,128)}, u32[]{:S(2)}) copy-start(f32[128,768]{1,0:T(8,128)} %copy-done.20) | copy-start | bytes 1179652
  398.7 95.6 %copy-start.25 = (bf16[128,768]{1,0:T(8,128)(2,1)S(1)}, bf16[128,768]{1,0:T(8,128)(2,1)}, u32[]{:S(2)}) copy-start(bf16[128,768]{1,0:T(8,128)(2,1)} %copy-done.23) | copy-start | bytes 589828
  398.7 95.6 %copy-start.37 = (f32[128,768]{1,0:T(8,128)S(1)}, f32[128,768]{1,0:T(8,128)}, u32[]{:S(2)}) copy-start(f32[128,768]{1,0:T(8,128)} %get-tuple-element.132) | copy-start | bytes 1179652
  398.7 95.6 %copy-start.62 = (f32[768]{0:T(1024)S(1)}, f32[768]{0:T(1024)}, u32[]{:S(2)}) copy-start(f32[768]{0:T(1024)} %copy-done.61) | copy-start | bytes 9220
  (64 other events, 187.9 us)
